TPU v7x, 1024 devices: a whole 8x8x8 slice. The times are simulated.
1024 devices in a mesh: group: 64 (over z_hi, y, core), shard: 16 (over z_lo, x).
Axes of the slice: x: 8, y: 8, z: 8 (z_hi: 4, z_lo: 2; z = z_hi * 2 + z_lo), core: 2. Of those that a mesh axis runs over, the one named last changes fastest.
Arguments:
- tokens: bfloat16 [20480, 3072], P(('group', 'shard')), may hold values from -6 to 6
- route_weight: bfloat16 [20480], P(('group', 'shard')), may hold values from 0.099609375 to 1
- counts: int32 [64], P('group'), may hold values from 80 to 320, as said below
- pulled: int32 [64], replicated, may hold values from 0 to 15
- weights: bfloat16 [16, 3072, 5376], P(None, 'group', 'shard'), may hold values from -0.109375 to 0.109375
- cotangent: bfloat16 [20480, 5376], P('group', 'shard'), may hold values from -6 to 6
Outputs:
- activated: bfloat16 [20480, 5376], P('group', 'shard')
- input_grads: bfloat16 [20480, 3072], P(('group', 'shard'))
- weight_grads: float32 [16, 3072, 5376], P(None, 'group', 'shard')
Inputs may be any that keep to these rules, and one draw needn't show every extreme that they name: `counts`: every draw has some group with all 320 slots live.
All inputs are finite; a program needn't handle non-finite values.
Results may differ from a plain program's by a relative error of at most 0.019.
Values may be sent and summed in bfloat16 or wider, within the bound.
A program may use at most 32 MiB of HBM per device.

v0:
```python
import jax
import jax.numpy as jnp
from jax import lax
from jax.sharding import PartitionSpec as P


def silu_parts(hidden):
    sigma = jax.nn.sigmoid(hidden)
    return (hidden * sigma, sigma * (1.0 + hidden * (1.0 - sigma)))


def shards(tokens, route_weight, counts, pulled, weights, cotangent):
    tok_rows, route_rows = (
        lax.all_gather(tokens, "shard", axis=0, tiled=True),
        lax.all_gather(route_weight, "shard", axis=0, tiled=True),
    )
    capacity = tok_rows.shape[0]
    features = tok_rows.shape[1]
    groups = lax.axis_size("group")
    outgoing = jnp.take(weights, pulled, axis=0)
    received = lax.all_to_all(outgoing, "group", split_axis=0, concat_axis=0, tiled=True)
    pulled_weight = received.reshape(features, received.shape[2])
    hidden = jnp.dot(tok_rows, pulled_weight, preferred_element_type=jnp.float32)
    valid_rows = jnp.arange(capacity, dtype=jnp.int32) < counts[0]
    weighting = jnp.where(valid_rows, route_rows.astype(jnp.float32), jnp.float32(0.0))[:, None]
    activated, derivative = silu_parts(hidden)
    output = (weighting * activated).astype(jnp.bfloat16)
    back_signal = (cotangent.astype(jnp.float32) * weighting * derivative).astype(jnp.bfloat16)
    input_grads = lax.psum_scatter(
        lax.dot_general(
            back_signal, pulled_weight, (((1,), (1,)), ((), ())), preferred_element_type=jnp.float32
        ).astype(jnp.bfloat16),
        "shard",
        scatter_dimension=0,
        tiled=True,
    )
    partial_value = lax.dot_general(
        tok_rows, back_signal, (((0,), (0,)), ((), ())), preferred_element_type=jnp.float32
    ).astype(jnp.bfloat16)
    blocks = partial_value.reshape(groups, weights.shape[1], weights.shape[2])
    returned = lax.all_to_all(blocks, "group", split_axis=0, concat_axis=0, tiled=True)
    owners = (pulled[None, :] == jnp.arange(weights.shape[0], dtype=jnp.int32)[:, None]).astype(
        jnp.bfloat16
    )
    summed = jnp.dot(owners, returned.reshape(groups, -1), preferred_element_type=jnp.float32)
    weight_grads = summed.reshape(weights.shape)
    return (output, input_grads, weight_grads)


def solution(mesh):
    in_specs = (
        P(("group", "shard"), None),
        P(("group", "shard")),
        P("group"),
        P(),
        P(None, "group", "shard"),
        P("group", "shard"),
    )
    out_specs = (P("group", "shard"), P(("group", "shard"), None), P(None, "group", "shard"))
    return jax.shard_map(shards, mesh=mesh, in_specs=in_specs, out_specs=out_specs, check_vma=False)
```

profile of v0, /device:TPU:12, one launch (start us, length us, event | category | flops | bytes accessed | tf_op | source)
XLA Modules:
  0.0 283.7 jit_solution(2898731793128799822)
XLA Ops:
  7.2 0.0 copy-start
  7.2 0.7 compare_select_fusion
  7.9 0.7 compare_and_fusion
  8.6 0.0 copy-done
  8.6 1.1 gather_fusion
  9.6 1.8 broadcast_select_fusion
  11.4 0.0 copy-start.5
  11.4 22.6 %all-to-all-start = ((bf16[64,48,336]{2,1,0:T(8,128)(2,1)}), bf16[64,48,336]{2,1,0:T(8,128)(2,1)S(1)}, u32[]{:S(2)}, u32[]{:S(2)}) async-start(bf16[64,48,336]{2,1,0:T(8,128)(2,1)} %broadcast_select_fusion), calls=%async_computation | async-start | bytes 4718592 | tf_op jit(solution)/shard_map/all_to_all | solution.py:21
  34.0 0.0 all-gather.3.cloned.1.call-start
  34.1 0.7 all-gather.3.cloned.1.call-update
  35.4 1.4 fusion.7
  37.5 0.0 copy-done.5
  37.5 0.2 dynamic-update-slice
  37.7 33.5 %all-reduce = bf16[320]{0:T(512)(128)(2,1)S(1)} all-reduce(bf16[320]{0:T(512)(128)(2,1)S(1)} %dynamic-update-slice), channel_id=1, replica_groups=mesh['group'=64,'shard'=16] {'shard'}, use_global_device_ids=true, to_apply=%add | all-reduce | flops 320 | bytes 1280
  71.2 58.8 %all-gather.3.cloned.1.call-done = bf16[16,20,3072]{2,1,0:T(8,128)(2,1)} async-done(((bf16[1,20,3072]{2,1,0:T(8,128)(2,1)}), bf16[16,20,3072]{2,1,0:T(8,128)(2,1)}) %all-gather.3.cloned.1.call-update) | async-done | bytes 1966096 | tf_op jit(solution)/shard_map/all_gather | solution.py:14
  130.1 3.9 %reshape.40 = bf16[320,3072]{1,0:T(8,128)(2,1)} reshape(bf16[16,20,3072]{2,1,0:T(8,128)(2,1)} %all-gather.3.cloned.1.call-done) | data formatting | bytes 3932160
  134.0 0.0 all-to-all-done
  134.0 0.0 copy-start.1
  134.0 0.0 copy-start.2
  134.0 0.0 copy-start.4
  134.0 4.4 %multiply_convert_fusion.1 = (bf16[320,336]{1,0:T(8,128)(2,1)}, f32[320,336]{1,0:T(8,128)S(1)}) fusion(f32[320]{0:T(512)S(1)} %convert_select_fusion, bf16[320,3072]{1,0:T(8,128)(2,1)} %reshape.40, bf16[3072,336]{1,0:T(8,128)(2,1)S(1)} %bitcast.25), kind=kOutput, calls=%fused_computation.9 | convolution fusion | flops 661248000 | bytes 4676864 | tf_op jit(solution)/shard_map/dot_general | solution.py:23
  138.4 0.0 copy-done.1
  138.4 0.0 copy-start.6
  138.4 0.8 copy-done.6
  139.2 0.0 copy-done.2
  139.2 0.0 copy-done.4
  139.2 1.4 fusion.1
  140.6 2.4 copy.13
  143.1 14.2 %all-to-all-start.1 = ((bf16[64,48,336]{2,1,0:T(8,128)(2,1)}), bf16[64,48,336]{2,1,0:T(8,128)(2,1)S(1)}, u32[]{:S(2)}, u32[]{:S(2)}) async-start(bf16[64,48,336]{2,1,0:T(8,128)(2,1)} %bitcast.23), calls=%async_computation.1 | async-start | bytes 4718592 | tf_op jit(solution)/shard_map/all_to_all | solution.py:41
  157.3 4.5 %convolution_convert_fusion.1 = bf16[320,3072]{1,0:T(8,128)(2,1)} fusion(bf16[3072,336]{1,0:T(8,128)(2,1)} %bitcast.26, f32[320,336]{1,0:T(8,128)} %copy-done.6, bf16[320,336]{1,0:T(8,128)(2,1)S(1)} %copy-done.4, f32[320]{0:T(512)S(1)} %convert_select_fusion), kind=kOutput, calls=%fused_computation.2 | convolution fusion | flops 662768640 | bytes 4676864 | tf_op jit(solution)/shard_map/dot_general | solution.py:30
  161.7 70.8 %fusion = bf16[24,3072]{1,0:T(8,128)(2,1)S(1)} fusion(bf16[320,3072]{1,0:T(8,128)(2,1)} %convolution_convert_fusion.1), kind=kCustom, calls=%all-reduce-scatter | all-reduce-scatter fusion | flops 1179649 | bytes 2117632
  232.6 8.7 %collective-permute-start.1 = (bf16[24,3072]{1,0:T(8,128)(2,1)S(1)}, bf16[24,3072]{1,0:T(8,128)(2,1)S(1)}, u32[]{:S(2)}, u32[]{:S(2)}) collective-permute-start(bf16[24,3072]{1,0:T(8,128)(2,1)S(1)} %fusion), channel_id=1, source_target_pairs={{0,2},{1,3},{2,4},{3,5},{4,6},{5,7},{6,8},{7,9},{8,10},{9,11},{10,... | collective-permute-start | bytes 442376
  241.3 4.3 %collective-permute-start = (bf16[24,3072]{1,0:T(8,128)(2,1)S(1)}, bf16[24,3072]{1,0:T(8,128)(2,1)S(1)}, u32[]{:S(2)}, u32[]{:S(2)}) collective-permute-start(bf16[24,3072]{1,0:T(8,128)(2,1)S(1)} %fusion), channel_id=1, source_target_pairs={{0,1},{1,2},{2,3},{3,4},{4,5},{5,6},{6,7},{7,8},{8,9},{9,10},{10,1... | collective-permute-start | bytes 442376
  245.7 0.7 slice.2
  246.3 1.9 collective-permute-start.2
  248.9 7.2 %collective-permute-done.2 = bf16[12,3072]{1,0:T(8,128)(2,1)S(1)} collective-permute-done((bf16[12,3072]{1,0:T(8,128)(2,1)}, bf16[12,3072]{1,0:T(8,128)(2,1)S(1)}, u32[]{:S(2)}, u32[]{:S(2)}) %collective-permute-start.2) | collective-permute-done | bytes 73760
  256.1 0.0 collective-permute-done.1
  256.1 0.0 collective-permute-done
  256.1 9.0 %concatenate = bf16[84,3072]{1,0:T(8,128)(2,1)} concatenate(bf16[12,3072]{1,0:T(8,128)(2,1)S(1)} %collective-permute-done.2, bf16[24,3072]{1,0:T(8,128)(2,1)S(1)} %collective-permute-done.1, bf16[24,3072]{1,0:T(8,128)(2,1)S(1)} %collective-permute-done, bf16[24,3072]{1,0:T(8,128)(2,1)S(1)} %fusion), dimensions={0} | concatenate | bytes 1032192
  265.1 1.6 constant_dynamic-slice_fusion
  266.8 0.0 all-to-all-done.1
  266.8 3.4 %reshape.26 = bf16[64,16128]{1,0:T(8,128)(2,1)} reshape(bf16[64,48,336]{2,1,0:T(8,128)(2,1)S(1)} %all-to-all-done.1) | data formatting | bytes 4128768 | tf_op jit(solution)/shard_map/reshape | solution.py:45
  270.1 0.0 copy-start.3
  270.1 4.8 %dot_general.23 = bf16[48,336,64]{1,0,2:T(8,128)(2,1)S(1)} reshape(bf16[16128,64]{0,1:T(8,128)(2,1)} %bitcast.24) | data formatting | bytes 4128768 | tf_op jit(solution)/shard_map/dot_general | solution.py:45
  274.9 0.0 copy-done.3
  275.0 0.5 fusion.2
  275.4 1.4 copy.15
  (3 shorter events, 0.0 us)
Async XLA Ops:
  7.2 1.4 copy-start
  11.4 26.1 %copy-start.5 = (bf16[20]{0:T(256)(128)(2,1)S(1)}, bf16[20]{0:T(256)(128)(2,1)}, u32[]{:S(2)}) copy-start(bf16[20]{0:T(256)(128)(2,1)} %param.7) | copy-start | bytes 124
  11.4 122.6 %all-to-all-start = ((bf16[64,48,336]{2,1,0:T(8,128)(2,1)}), bf16[64,48,336]{2,1,0:T(8,128)(2,1)S(1)}, u32[]{:S(2)}, u32[]{:S(2)}) async-start(bf16[64,48,336]{2,1,0:T(8,128)(2,1)} %broadcast_select_fusion), calls=%async_computation | async-start | bytes 4718592 | tf_op jit(solution)/shard_map/all_to_all | solution.py:21
  34.0 96.0 %all-gather.3.cloned.1.call-start = ((), (), s32[]{:S(2)}) async-start(), calls=%async_computation.2 | async-start | bytes 2506752 | tf_op jit(solution)/shard_map/all_gather | solution.py:14
  134.0 4.4 %copy-start.1 = (bf16[64,48,336]{2,1,0:T(8,128)(2,1)}, bf16[64,48,336]{2,1,0:T(8,128)(2,1)S(1)}, u32[]{:S(2)}) copy-start(bf16[64,48,336]{2,1,0:T(8,128)(2,1)S(1)} %all-to-all-done) | copy-start | bytes 6193156
  134.0 5.2 %copy-start.2 = (bf16[320,3072]{1,0:T(8,128)(2,1)S(1)}, bf16[320,3072]{1,0:T(8,128)(2,1)}, u32[]{:S(2)}) copy-start(bf16[320,3072]{1,0:T(8,128)(2,1)} %reshape.40) | copy-start | bytes 5898244
  134.0 5.2 %copy-start.4 = (bf16[320,336]{1,0:T(8,128)(2,1)S(1)}, bf16[320,336]{1,0:T(8,128)(2,1)}, u32[]{:S(2)}) copy-start(bf16[320,336]{1,0:T(8,128)(2,1)} %param.11) | copy-start | bytes 645124
  138.4 0.8 copy-start.6
  143.1 123.7 %all-to-all-start.1 = ((bf16[64,48,336]{2,1,0:T(8,128)(2,1)}), bf16[64,48,336]{2,1,0:T(8,128)(2,1)S(1)}, u32[]{:S(2)}, u32[]{:S(2)}) async-start(bf16[64,48,336]{2,1,0:T(8,128)(2,1)} %bitcast.23), calls=%async_computation.1 | async-start | bytes 4718592 | tf_op jit(solution)/shard_map/all_to_all | solution.py:41
  232.6 23.5 %collective-permute-start.1 = (bf16[24,3072]{1,0:T(8,128)(2,1)S(1)}, bf16[24,3072]{1,0:T(8,128)(2,1)S(1)}, u32[]{:S(2)}, u32[]{:S(2)}) collective-permute-start(bf16[24,3072]{1,0:T(8,128)(2,1)S(1)} %fusion), channel_id=1, source_target_pairs={{0,2},{1,3},{2,4},{3,5},{4,6},{5,7},{6,8},{7,9},{8,10},{9,11},{10,... | collective-permute-start | bytes 442376
  241.3 14.8 %collective-permute-start = (bf16[24,3072]{1,0:T(8,128)(2,1)S(1)}, bf16[24,3072]{1,0:T(8,128)(2,1)S(1)}, u32[]{:S(2)}, u32[]{:S(2)}) collective-permute-start(bf16[24,3072]{1,0:T(8,128)(2,1)S(1)} %fusion), channel_id=1, source_target_pairs={{0,1},{1,2},{2,3},{3,4},{4,5},{5,6},{6,7},{7,8},{8,9},{9,10},{10,1... | collective-permute-start | bytes 442376
  246.3 9.8 %collective-permute-start.2 = (bf16[12,3072]{1,0:T(8,128)(2,1)}, bf16[12,3072]{1,0:T(8,128)(2,1)S(1)}, u32[]{:S(2)}, u32[]{:S(2)}) collective-permute-start(bf16[12,3072]{1,0:T(8,128)(2,1)} %slice.2), channel_id=1, source_target_pairs={{0,3},{1,4},{2,5},{3,6},{4,7},{5,8},{6,9},{7,10},{8,11},{9,12},{10... | collective-permute-start | bytes 221192
  270.1 4.8 %copy-start.3 = (s32[64]{0:T(128)S(1)}, s32[64]{0:T(128)}, u32[]{:S(2)}) copy-start(s32[64]{0:T(128)} %param.9) | copy-start | bytes 772
Sparse Core Ops, SparseCore 0:
  37.5 92.4 all-gather.2
where the time goes:
time: 285 us; the launch traced here: 284 us
  blocking collectives  104 us (36%)
  waiting for transfers between devices  66.7 us (23%)
  starting transfers between devices  51.8 us (18%)
  local copies, waits for them, and re-layouts  30.8 us (11%)
  between operations  16.1 us (6%)
  matrix products  10.7 us (4%)
  other arithmetic  3.15 us (1%)
    unnamed x2, blocking collectives  104 us
    all_gather x1, waiting for transfers between devices, shards(): lax.all_gather(tokens, 'shard', axis=0, tiled=True)  58.8 us
    all_to_all x1, starting transfers between devices, shards(): lax.all_to_all(outgoing, 'group', split_axis=0, concat_axis=0, tiled=True)  22.6 us
    unnamed x22, local copies, waits for them, and re-layouts  19.1 us
    unnamed x3, starting transfers between devices  15 us
    all_to_all x1, starting transfers between devices, shards(): lax.all_to_all(blocks, 'group', split_axis=0, concat_axis=0, tiled=True)  14.2 us
    unnamed x4, waiting for transfers between devices  7.89 us
  transfers between devices with their start and end apart: 6, of which 2 were waited for; matrix products, arithmetic and copies ran while one was open for 33% of the time, Pallas kernels for 0%

commit v1 on v0

v1 whole, which is shorter than its diff:
```python
import functools

import jax
import jax.numpy as jnp
from jax import lax
from jax.experimental import pallas as pl
from jax.experimental.pallas import tpu as pltpu
from jax.sharding import PartitionSpec as P

MESH = pl.DeviceIdType.MESH
NZ, NY, NC, NX = 4, 8, 2, 8
ROWS, COLS, TOK = 48, 336, 20
CAP, D = 320, 3072
KC = 8
KW = D // KC
BF, F32 = jnp.bfloat16, jnp.float32
ORDER_Y = (1, 7, 2, 6, 3, 5, 4)
ORDER_Z = (1, 3, 2)


def pack(wide):
    n = wide.shape[0]
    tail = wide[:, :, 256:]
    lane = lax.broadcasted_iota(jnp.int32, (n, 16, 128), 2)
    last = tail[:, 32:48]
    low = jnp.where(lane < 80, tail[:, 0:16], pltpu.roll(last, 80, 2))
    high = jnp.where(lane < 80, tail[:, 16:32], pltpu.roll(last, 32, 2))
    return jnp.concatenate([wide[:, :, 0:128], wide[:, :, 128:256], low, high], axis=1)


def unpack_tail(tail):
    n = tail.shape[0]
    lane = lax.broadcasted_iota(jnp.int32, (n, 16, 128), 2)
    zero = jnp.zeros((n, 16, 128), F32)
    low, high = tail[:, 0:16], tail[:, 16:32]
    last = jnp.where(lane < 48, pltpu.roll(low, 48, 2), jnp.where(lane < 80, pltpu.roll(high, 96, 2), zero))
    return jnp.concatenate([jnp.where(lane < 80, low, zero), jnp.where(lane < 80, high, zero), last], axis=1)


def main_kernel(
    pulled, counts, tok, route, weights, cot,
    act_out, dx_out, grad_out,
    packed, send_a, send_b, mid_a, mid_b, land, full,
    back_a, back_b, bmid_a, bmid_b,
    own_tok, pair_tok, ring, xk, xt, scale, cotp, hid, sig,
    terms, got, zsend, zrecv, half,
    w1a, w1b, w2, wl, g1a, g1b, g2, gl, ps, rg, xs,
):
    g, s = lax.axis_index("group"), lax.axis_index("shard")
    zh, y, c = g // 16, lax.rem(g // 2, NY), lax.rem(g, 2)
    zl, x = s // NX, lax.rem(s, NX)

    def gdev(zh_, y_, c_):
        return ((zh_ * NY + y_) * 2 + c_, s)

    def sdev(zl_, x_):
        return (g, zl_ * NX + x_)

    bar = pltpu.get_barrier_semaphore()

    def greet(dev):
        pl.semaphore_signal(bar, inc=1, device_id=dev, device_id_type=MESH)

    for dy in range(1, NY):
        greet(gdev(zh, lax.rem(y + dy, NY), c))
        greet(gdev(zh, lax.rem(y + dy, NY), 1 - c))
    for dz in range(1, NZ):
        greet(gdev(lax.rem(zh + dz, NZ), y, c))
        greet(gdev(lax.rem(zh + dz, NZ), y, 1 - c))
    greet(gdev(zh, y, 1 - c))
    for dx in range(1, NX):
        greet(sdev(zl, lax.rem(x + dx, NX)))
    greet(sdev(1 - zl, x))

    own_tok[:, 0:D] = tok[...]
    own_tok[:, D:] = route[...]

    def pack_one(e, carry):
        wide = jnp.concatenate([weights[e].astype(F32), jnp.zeros((ROWS, 384 - COLS), F32)], axis=1)
        packed[e] = pack(wide[None])[0].astype(BF)
        return carry

    lax.fori_loop(0, weights.shape[0], pack_one, 0)

    def fill(k, carry):
        zt, yt = k // NY, lax.rem(k, NY)
        send_a[yt, zt] = packed[pulled[2 * k]]
        send_b[zt, yt] = packed[pulled[2 * k + 1]]
        return carry

    lax.fori_loop(0, NZ * NY, fill, 0)

    pl.semaphore_wait(bar, 29)

    def exchange(src_a, src_b, ia, ib, dst, s1a, s1b, s2, sl):
        def a1(dy):
            yt = lax.rem(y + dy, NY)
            return pltpu.make_async_remote_copy(
                src_a.at[yt], ia.at[y], s1a.at[0, dy], s1a.at[1, dy], device_id=gdev(zh, yt, c), device_id_type=MESH)

        def b1(dz):
            zt = lax.rem(zh + dz, NZ)
            return pltpu.make_async_remote_copy(
                src_b.at[zt], ib.at[zh], s1b.at[0, dz], s1b.at[1, dz], device_id=gdev(zt, y, c), device_id_type=MESH)

        def a2(dz, cross):
            zt = lax.rem(zh + dz, NZ)
            k = dz * 2 + cross
            return pltpu.make_async_remote_copy(
                ia.at[:, zt], dst.at[zh, :, c], s2.at[0, k], s2.at[1, k], device_id=gdev(zt, y, 0), device_id_type=MESH)

        def b2(dy, cross):
            yt = lax.rem(y + dy, NY)
            k = dy * 2 + cross
            return pltpu.make_async_remote_copy(
                ib.at[:, yt], dst.at[:, y, c], s2.at[0, k], s2.at[1, k], device_id=gdev(zh, yt, 1), device_id_type=MESH)

        la = pltpu.make_async_copy(src_a.at[y], ia.at[y], sl.at[0])
        lb = pltpu.make_async_copy(src_b.at[zh], ib.at[zh], sl.at[1])
        l2a = pltpu.make_async_copy(ia.at[:, zh], dst.at[zh, :, 0], sl.at[2])
        l2b = pltpu.make_async_copy(ib.at[:, y], dst.at[:, y, 1], sl.at[2])

        def start1():
            la.start()
            lb.start()
            for i, dy in enumerate(ORDER_Y):
                a1(dy).start()
                if i % 2 == 0 and i // 2 < 3:
                    b1(ORDER_Z[i // 2]).start()

        def turn_a():
            la.wait()
            for dy in ORDER_Y:
                a1(dy).wait()

            @pl.when(c == 0)
            def _():
                l2a.start()
                for dz in ORDER_Z:
                    a2(dz, 0).start()

            @pl.when(c == 1)
            def _():
                for dz in ORDER_Z + (0,):
                    a2(dz, 1).start()

        def turn_b():
            lb.wait()
            for dz in ORDER_Z:
                b1(dz).wait()

            @pl.when(c == 1)
            def _():
                l2b.start()
                for dy in ORDER_Y:
                    b2(dy, 0).start()

            @pl.when(c == 0)
            def _():
                for dy in ORDER_Y + (0,):
                    b2(dy, 1).start()

        def finish():
            @pl.when(c == 0)
            def _():
                l2a.wait()
                for dz in ORDER_Z:
                    a2(dz, 0).wait()
                for dz in ORDER_Z + (0,):
                    a2(dz, 1).wait_recv()
                for dy in ORDER_Y + (0,):
                    b2(dy, 1).wait_send()

            @pl.when(c == 1)
            def _():
                l2b.wait()
                for dy in ORDER_Y:
                    b2(dy, 0).wait()
                for dy in ORDER_Y + (0,):
                    b2(dy, 1).wait_recv()
                for dz in ORDER_Z + (0,):
                    a2(dz, 1).wait_send()

        return start1, turn_a, turn_b, finish

    pair = pltpu.make_async_remote_copy(
        own_tok, pair_tok, ps.at[0], ps.at[1], device_id=sdev(1 - zl, x), device_id_type=MESH)
    pair.start()
    w_start1, w_turn_a, w_turn_b, w_finish = exchange(
        send_a, send_b, mid_a, mid_b, land, w1a, w1b, w2, wl)
    w_start1()

    pair.wait()
    mine, other = own_tok[...].astype(F32), pair_tok[...].astype(F32)
    ring[x] = jnp.concatenate(
        [jnp.where(zl == 0, mine, other), jnp.where(zl == 0, other, mine)], axis=0).astype(BF)

    right, left = lax.rem(x + 1, NX), lax.rem(x + NX - 1, NX)
    cut = 13 * 128

    def hop(step):
        a, b = lax.rem(x - step + 1 + NX, NX), lax.rem(x + step - 1, NX)
        if step < 4:
            ra, rb = ring.at[a], ring.at[b]
        else:
            ra, rb = ring.at[a, :, 0:cut], ring.at[b, :, cut:]
        k = 2 * (step - 1)
        return (
            pltpu.make_async_remote_copy(
                ra, ra, rg.at[0, k], rg.at[1, k], device_id=sdev(zl, right), device_id_type=MESH),
            pltpu.make_async_remote_copy(
                rb, rb, rg.at[0, k + 1], rg.at[1, k + 1], device_id=sdev(zl, left), device_id_type=MESH),
        )

    def hop_start(step):
        for copy in hop(step):
            copy.start()

    def hop_wait(step):
        for copy in hop(step):
            copy.wait()

    hop_start(1)
    cotp[:, 256:] = jnp.zeros((CAP, 128), F32)
    cotp[:, 0:COLS] = cot[...].astype(F32)
    hop_wait(1)
    hop_start(2)
    hop_wait(2)
    hop_start(3)
    w_turn_a()
    w_turn_b()
    hop_wait(3)
    hop_start(4)
    hop_wait(4)

    def gather_rows(lanes):
        parts = [ring[i, :, lanes].astype(F32) for i in range(NX)]
        return jnp.concatenate([p[0:TOK] for p in parts] + [p[TOK:] for p in parts], axis=0)

    def order(k, carry):
        rows = gather_rows(pl.ds(pl.multiple_of(k * KW, 128), KW))
        xk[k] = rows.astype(BF)
        xt[k] = rows.T.astype(BF)
        return carry

    lax.fori_loop(0, KC, order, 0)
    live = lax.broadcasted_iota(jnp.int32, (CAP, 128), 0) < counts[0]
    scale[...] = jnp.where(live, gather_rows(pl.ds(D, 128)), jnp.zeros((CAP, 128), F32))
    hid[...] = jnp.zeros((CAP, 384), F32)

    w_finish()

    def forward(k, carry):
        blocks = land[k // 2, pl.ds(lax.rem(k, 2) * 4, 4)].reshape(8, 128, 128)
        tail = unpack_tail(blocks[:, 96:].astype(F32)).reshape(KW, 128).astype(BF)
        chunk = jnp.concatenate(
            [blocks[:, 0:ROWS].reshape(KW, 128), blocks[:, ROWS:2 * ROWS].reshape(KW, 128), tail], axis=1)
        full[k] = chunk
        hid[...] += jnp.dot(xk[k], chunk, preferred_element_type=F32)
        return carry

    lax.fori_loop(0, KC, forward, 0)

    for t in range(3):
        lanes = slice(128 * t, 128 * t + 128)
        h, sc = hid[:, lanes], scale[...]
        sigma = jax.nn.sigmoid(h)
        value = (sc * (h * sigma)).astype(BF)
        if t < 2:
            act_out[:, lanes] = value
        else:
            act_out[:, 256:COLS] = value[:, 0:80]
        sig[:, lanes] = (cotp[:, lanes] * sc * (sigma * (1.0 + h * (1.0 - sigma)))).astype(BF)

    def grads(k, carry):
        part = jnp.dot(xt[k], sig[...], preferred_element_type=F32)
        blocks = pack(part.reshape(8, ROWS, 384)).astype(BF)
        zt, y0 = k // 2, lax.rem(k, 2) * 4
        for j in range(4):
            back_a[y0 + j, zt] = blocks[2 * j]
            back_b[zt, y0 + j] = blocks[2 * j + 1]
        return carry

    lax.fori_loop(0, KC, grads, 0)
    g_start1, g_turn_a, g_turn_b, g_finish = exchange(
        back_a, back_b, bmid_a, bmid_b, grad_out, g1a, g1b, g2, gl)
    g_start1()

    def inputs(k, carry):
        term = lax.dot_general(sig[...], full[k], (((1,), (1,)), ((), ())), preferred_element_type=F32)
        lanes = pl.ds(pl.multiple_of(k * KW, 128), KW)
        for i in range(NX):
            terms[i, :, lanes] = jnp.concatenate(
                [term[TOK * i:TOK * i + TOK], term[160 + TOK * i:160 + TOK * i + TOK]], axis=0).astype(BF)
        return carry

    lax.fori_loop(0, KC, inputs, 0)

    def xcopy(dx):
        xt_ = lax.rem(x + dx, NX)
        return pltpu.make_async_remote_copy(
            terms.at[xt_], got.at[x], xs.at[0, dx], xs.at[1, dx], device_id=sdev(zl, xt_), device_id_type=MESH)

    for dx in ORDER_Y:
        xcopy(dx).start()
    got[x] = terms[x]

    g_turn_a()
    g_turn_b()
    for dx in ORDER_Y:
        xcopy(dx).wait()

    def add_up(k, carry):
        lanes = pl.ds(pl.multiple_of(k * KW, 128), KW)
        total = got[0, :, lanes].astype(F32)
        for i in range(1, NX):
            total = total + got[i, :, lanes].astype(F32)
        low, high = total[0:TOK], total[TOK:]
        half[:, lanes] = jnp.where(zl == 0, low, high)
        zsend[:, lanes] = jnp.where(zl == 0, high, low).astype(BF)
        return carry

    lax.fori_loop(0, KC, add_up, 0)
    last = pltpu.make_async_remote_copy(
        zsend, zrecv, ps.at[2], ps.at[3], device_id=sdev(1 - zl, x), device_id_type=MESH)
    last.start()
    last.wait()
    dx_out[...] = (half[...] + zrecv[...].astype(F32)).astype(BF)
    g_finish()


def sum_kernel(pulled, blocks, out, acc):
    acc[...] = jnp.zeros(acc.shape, F32)

    def add(k, carry):
        e = pulled[k]
        acc[e] = acc[e] + blocks[k].astype(F32)
        return carry

    lax.fori_loop(0, blocks.shape[0], add, 0)

    def spread(e, carry):
        total = acc[e]
        out[e, :, 0:128] = total[0:ROWS]
        out[e, :, 128:256] = total[ROWS:2 * ROWS]
        out[e, :, 256:COLS] = unpack_tail(total[None, 96:])[0, :, 0:80]
        return carry

    lax.fori_loop(0, out.shape[0], spread, 0)


def shards(tokens, route_weight, counts, pulled, weights, cotangent):
    vmem, smem = pl.BlockSpec(memory_space=pltpu.VMEM), pl.BlockSpec(memory_space=pltpu.SMEM)
    dma = pltpu.SemaphoreType.DMA
    route = jnp.broadcast_to(route_weight[:, None], (TOK, 128))
    activated, input_grads, blocks = pl.pallas_call(
        main_kernel,
        out_shape=[
            jax.ShapeDtypeStruct((CAP, COLS), BF),
            jax.ShapeDtypeStruct((TOK, D), BF),
            jax.ShapeDtypeStruct((NZ, NY, NC, 128, 128), BF),
        ],
        in_specs=[smem, smem, vmem, vmem, vmem, vmem],
        out_specs=[vmem, vmem, vmem],
        scratch_shapes=[
            pltpu.VMEM((16, 128, 128), BF),
            pltpu.VMEM((NY, NZ, 128, 128), BF),
            pltpu.VMEM((NZ, NY, 128, 128), BF),
            pltpu.VMEM((NY, NZ, 128, 128), BF),
            pltpu.VMEM((NZ, NY, 128, 128), BF),
            pltpu.VMEM((NZ, NY, NC, 128, 128), BF),
            pltpu.VMEM((KC, KW, 384), BF),
            pltpu.VMEM((NY, NZ, 128, 128), BF),
            pltpu.VMEM((NZ, NY, 128, 128), BF),
            pltpu.VMEM((NY, NZ, 128, 128), BF),
            pltpu.VMEM((NZ, NY, 128, 128), BF),
            pltpu.VMEM((TOK, D + 128), BF),
            pltpu.VMEM((TOK, D + 128), BF),
            pltpu.VMEM((NX, 2 * TOK, D + 128), BF),
            pltpu.VMEM((KC, CAP, KW), BF),
            pltpu.VMEM((KC, KW, CAP), BF),
            pltpu.VMEM((CAP, 128), F32),
            pltpu.VMEM((CAP, 384), F32),
            pltpu.VMEM((CAP, 384), F32),
            pltpu.VMEM((CAP, 384), BF),
            pltpu.VMEM((NX, 2 * TOK, D), BF),
            pltpu.VMEM((NX, 2 * TOK, D), BF),
            pltpu.VMEM((TOK, D), BF),
            pltpu.VMEM((TOK, D), BF),
            pltpu.VMEM((TOK, D), F32),
            dma((2, NY)), dma((2, NZ)), dma((2, 2 * NY)), dma((3,)),
            dma((2, NY)), dma((2, NZ)), dma((2, 2 * NY)), dma((3,)),
            dma((4,)), dma((2, 8)), dma((2, NX)),
        ],
        compiler_params=pltpu.CompilerParams(
            collective_id=1, has_side_effects=True, vmem_limit_bytes=50 << 20),
        name="exchange_and_compute",
    )(pulled, counts, tokens, route, weights, cotangent)
    weight_grads = pl.pallas_call(
        sum_kernel,
        out_shape=jax.ShapeDtypeStruct(weights.shape, F32),
        in_specs=[smem, vmem],
        out_specs=vmem,
        scratch_shapes=[pltpu.VMEM((weights.shape[0], 128, 128), F32)],
        compiler_params=pltpu.CompilerParams(vmem_limit_bytes=24 << 20),
        name="sum_per_expert",
    )(pulled, blocks.reshape(NZ * NY * NC, 128, 128))
    return activated, input_grads, weight_grads


def solution(mesh):
    in_specs = (
        P(("group", "shard"), None),
        P(("group", "shard")),
        P("group"),
        P(),
        P(None, "group", "shard"),
        P("group", "shard"),
    )
    out_specs = (P("group", "shard"), P(("group", "shard"), None), P(None, "group", "shard"))
    return jax.shard_map(shards, mesh=mesh, in_specs=in_specs, out_specs=out_specs, check_vma=False)
```

time: 285 us -> 146 us (0.51)
  the two profiles are of different devices: /device:TPU:12 before, /device:TPU:1 now
where the time goes in v1:
time: 146 us
  Pallas kernels  139 us (95%)
  local copies, waits for them, and re-layouts  5.65 us (4%)
    pallas_call x1, Pallas kernels, shards(): pl.pallas_call(main_kernel, out_shape=[jax.ShapeDtypeStruct((CAP, COLS),...  135 us
    unnamed x10, local copies, waits for them, and re-layouts  4.93 us
    pallas_call x1, Pallas kernels, shards(): pl.pallas_call(sum_kernel, out_shape=jax.ShapeDtypeStruct(weights.shape,...  3.52 us

profile of v1, /device:TPU:1, one launch (start us, length us, event | category | flops | bytes accessed | tf_op | source)
XLA Modules:
  0.0 145.6 jit_solution(1779080308812801850)
XLA Ops:
  1.3 0.7 broadcast_in_dim.2.route
  2.0 0.0 copy-start
  2.0 1.1 copy-done
  3.1 0.0 copy-start.1
  3.1 0.9 copy-done.1
  4.0 0.0 copy-start.2
  4.0 0.9 copy-done.2
  4.9 0.0 copy-start.3
  4.9 0.7 copy-done.3
  5.6 135.1 %exchange_and_compute.1 = (bf16[320,336]{1,0:T(8,128)(2,1)S(1)}, bf16[20,3072]{1,0:T(8,128)(2,1)S(1)}, bf16[4,8,2,128,128]{4,3,2,1,0:T(8,128)(2,1)S(1)}) custom-call(s32[64]{0:T(128)S(1)} %copy-done.3, s32[1]{0:T(128)S(6)} %copy.11.counts, bf16[20,3072]{1,0:T(8,128)(2,1)S(1)} %copy-done.2, bf16[20,128]{1,0:T(8,128)(2,1)S(1)} %broadcast_in_dim.2.route, ...), custom_call_target="tpu_custom_call" | custom-call | tf_op jit(solution)/shard_map/exchange_and_compute/pallas_call | solution.py:356
  140.7 3.5 %sum_per_expert.1 = f32[16,48,336]{2,1,0:T(8,128)} custom-call(s32[64]{0:T(128)S(1)} %copy-done.3, bf16[64,128,128]{2,1,0:T(8,128)(2,1)S(1)} %bitcast.1), custom_call_target="tpu_custom_call" | custom-call | tf_op jit(solution)/shard_map/sum_per_expert/pallas_call | solution.py:399
  144.2 0.7 copy.12
  144.9 0.7 copy.13
Async XLA Ops:
  2.0 1.1 copy-start
  3.1 0.9 copy-start.1
  4.0 0.9 copy-start.2
  4.9 0.7 copy-start.3

commit v2 on v1

--- a/solution.py
+++ b/solution.py
@@ -18,14 +18,13 @@
 ORDER_Z = (1, 3, 2)
 
 
-def pack(wide):
-    n = wide.shape[0]
-    tail = wide[:, :, 256:]
+def pack_tail(tail):
+    n = tail.shape[0]
     lane = lax.broadcasted_iota(jnp.int32, (n, 16, 128), 2)
     last = tail[:, 32:48]
     low = jnp.where(lane < 80, tail[:, 0:16], pltpu.roll(last, 80, 2))
     high = jnp.where(lane < 80, tail[:, 16:32], pltpu.roll(last, 32, 2))
-    return jnp.concatenate([wide[:, :, 0:128], wide[:, :, 128:256], low, high], axis=1)
+    return jnp.concatenate([low, high], axis=1)
 
 
 def unpack_tail(tail):
@@ -38,13 +37,15 @@
 
 
 def main_kernel(
-    pulled, counts, tok, route, weights, cot,
+    pulled, counts, tok_hbm, route_hbm, weights_hbm, cot_hbm,
     act_out, dx_out, grad_out,
-    packed, send_a, send_b, mid_a, mid_b, land, full,
-    back_a, back_b, bmid_a, bmid_b,
-    own_tok, pair_tok, ring, xk, xt, scale, cotp, hid, sig,
+    weights, cot, packed1, packed2,
+    sa1, sb1, ma1, mb1, land1, sa2, sb2, ma2, mb2, land2, full,
+    ba1, bb1, na1, nb1, back1, ba2, bb2, na2, nb2, back2,
+    own_tok, pair_tok, ring, xk, xt, scale, cotp, hid, sig, pick,
     terms, got, zsend, zrecv, half,
-    w1a, w1b, w2, wl, g1a, g1b, g2, gl, ps, rg, xs,
+    p1a, p1b, p2, pl_, q1a, q1b, q2, ql_, r1a, r1b, r2, rl_, t1a, t1b, t2, tl_,
+    ps, rg, xs, ins,
 ):
     g, s = lax.axis_index("group"), lax.axis_index("shard")
     zh, y, c = g // 16, lax.rem(g // 2, NY), lax.rem(g, 2)
@@ -55,6 +56,15 @@
 
     def sdev(zl_, x_):
         return (g, zl_ * NX + x_)
+
+    loads = [
+        pltpu.make_async_copy(weights_hbm, weights, ins.at[0]),
+        pltpu.make_async_copy(tok_hbm, own_tok.at[:, 0:D], ins.at[1]),
+        pltpu.make_async_copy(route_hbm, own_tok.at[:, D:], ins.at[2]),
+        pltpu.make_async_copy(cot_hbm, cot, ins.at[3]),
+    ]
+    for load in loads:
+        load.start()
 
     bar = pltpu.get_barrier_semaphore()
 
@@ -72,23 +82,27 @@
         greet(sdev(zl, lax.rem(x + dx, NX)))
     greet(sdev(1 - zl, x))
 
-    own_tok[:, 0:D] = tok[...]
-    own_tok[:, D:] = route[...]
+    loads[0].wait()
 
     def pack_one(e, carry):
-        wide = jnp.concatenate([weights[e].astype(F32), jnp.zeros((ROWS, 384 - COLS), F32)], axis=1)
-        packed[e] = pack(wide[None])[0].astype(BF)
+        packed1[e] = jnp.concatenate([weights[e, :, 0:128], weights[e, :, 128:256]], axis=0)
+        tail = jnp.concatenate([weights[e, :, 256:].astype(F32), jnp.zeros((ROWS, 384 - COLS), F32)], axis=1)
+        packed2[e] = pack_tail(tail[None])[0].astype(BF)
         return carry
 
     lax.fori_loop(0, weights.shape[0], pack_one, 0)
 
     def fill(k, carry):
         zt, yt = k // NY, lax.rem(k, NY)
-        send_a[yt, zt] = packed[pulled[2 * k]]
-        send_b[zt, yt] = packed[pulled[2 * k + 1]]
+        sa1[yt, zt] = packed1[pulled[2 * k]]
+        sb1[zt, yt] = packed1[pulled[2 * k + 1]]
+        sa2[yt, zt] = packed2[pulled[2 * k]]
+        sb2[zt, yt] = packed2[pulled[2 * k + 1]]
         return carry
 
     lax.fori_loop(0, NZ * NY, fill, 0)
+    loads[1].wait()
+    loads[2].wait()
 
     pl.semaphore_wait(bar, 29)
 
@@ -186,9 +200,10 @@
     pair = pltpu.make_async_remote_copy(
         own_tok, pair_tok, ps.at[0], ps.at[1], device_id=sdev(1 - zl, x), device_id_type=MESH)
     pair.start()
-    w_start1, w_turn_a, w_turn_b, w_finish = exchange(
-        send_a, send_b, mid_a, mid_b, land, w1a, w1b, w2, wl)
-    w_start1()
+    w1 = exchange(sa1, sb1, ma1, mb1, land1, p1a, p1b, p2, pl_)
+    w2 = exchange(sa2, sb2, ma2, mb2, land2, q1a, q1b, q2, ql_)
+    w1[0]()
+    w2[0]()
 
     pair.wait()
     mine, other = own_tok[...].astype(F32), pair_tok[...].astype(F32)
@@ -221,16 +236,29 @@
             copy.wait()
 
     hop_start(1)
+    loads[3].wait()
     cotp[:, 256:] = jnp.zeros((CAP, 128), F32)
     cotp[:, 0:COLS] = cot[...].astype(F32)
+
+    column = lax.broadcasted_iota(jnp.int32, (1, 1024), 1)
+    expert = jnp.zeros((1, 1024), jnp.int32)
+    for k in range(NZ * NY * NC):
+        expert = jnp.where(column // 16 == k, pulled[k], expert)
+    for e in range(16):
+        row = lax.broadcasted_iota(jnp.int32, (16, 1024), 0)
+        hit = (row == lax.rem(column, 16)) & (expert == e)
+        pick[16 * e:16 * e + 16] = jnp.where(hit, jnp.float32(1), jnp.float32(0)).astype(BF)
+
     hop_wait(1)
     hop_start(2)
     hop_wait(2)
     hop_start(3)
-    w_turn_a()
-    w_turn_b()
+    w1[1]()
+    w1[2]()
     hop_wait(3)
     hop_start(4)
+    w2[1]()
+    w2[2]()
     hop_wait(4)
 
     def gather_rows(lanes):
@@ -248,20 +276,7 @@
     scale[...] = jnp.where(live, gather_rows(pl.ds(D, 128)), jnp.zeros((CAP, 128), F32))
     hid[...] = jnp.zeros((CAP, 384), F32)
 
-    w_finish()
-
-    def forward(k, carry):
-        blocks = land[k // 2, pl.ds(lax.rem(k, 2) * 4, 4)].reshape(8, 128, 128)
-        tail = unpack_tail(blocks[:, 96:].astype(F32)).reshape(KW, 128).astype(BF)
-        chunk = jnp.concatenate(
-            [blocks[:, 0:ROWS].reshape(KW, 128), blocks[:, ROWS:2 * ROWS].reshape(KW, 128), tail], axis=1)
-        full[k] = chunk
-        hid[...] += jnp.dot(xk[k], chunk, preferred_element_type=F32)
-        return carry
-
-    lax.fori_loop(0, KC, forward, 0)
-
-    for t in range(3):
+    def activate(t):
         lanes = slice(128 * t, 128 * t + 128)
         h, sc = hid[:, lanes], scale[...]
         sigma = jax.nn.sigmoid(h)
@@ -272,19 +287,59 @@
             act_out[:, 256:COLS] = value[:, 0:80]
         sig[:, lanes] = (cotp[:, lanes] * sc * (sigma * (1.0 + h * (1.0 - sigma)))).astype(BF)
 
-    def grads(k, carry):
-        part = jnp.dot(xt[k], sig[...], preferred_element_type=F32)
-        blocks = pack(part.reshape(8, ROWS, 384)).astype(BF)
+    w1[3]()
+
+    def forward1(k, carry):
+        blocks = land1[k // 2, pl.ds(lax.rem(k, 2) * 4, 4)].reshape(8, 96, 128)
+        chunk = jnp.concatenate(
+            [blocks[:, 0:ROWS].reshape(KW, 128), blocks[:, ROWS:].reshape(KW, 128)], axis=1)
+        full[k, :, 0:256] = chunk
+        hid[:, 0:256] += jnp.dot(xk[k], chunk, preferred_element_type=F32)
+        return carry
+
+    lax.fori_loop(0, KC, forward1, 0)
+    activate(0)
+    activate(1)
+
+    def grads1(k, carry):
+        part = jnp.dot(xt[k], sig[:, 0:256], preferred_element_type=F32).astype(BF)
+        low, high = part[:, 0:128].reshape(8, ROWS, 128), part[:, 128:].reshape(8, ROWS, 128)
         zt, y0 = k // 2, lax.rem(k, 2) * 4
         for j in range(4):
-            back_a[y0 + j, zt] = blocks[2 * j]
-            back_b[zt, y0 + j] = blocks[2 * j + 1]
-        return carry
-
-    lax.fori_loop(0, KC, grads, 0)
-    g_start1, g_turn_a, g_turn_b, g_finish = exchange(
-        back_a, back_b, bmid_a, bmid_b, grad_out, g1a, g1b, g2, gl)
-    g_start1()
+            ba1[y0 + j, zt, 0:ROWS] = low[2 * j]
+            ba1[y0 + j, zt, ROWS:] = high[2 * j]
+            bb1[zt, y0 + j, 0:ROWS] = low[2 * j + 1]
+            bb1[zt, y0 + j, ROWS:] = high[2 * j + 1]
+        return carry
+
+    lax.fori_loop(0, KC, grads1, 0)
+    g1 = exchange(ba1, bb1, na1, nb1, back1, r1a, r1b, r2, rl_)
+    g1[0]()
+
+    w2[3]()
+
+    def forward2(k, carry):
+        blocks = land2[k // 2, pl.ds(lax.rem(k, 2) * 4, 4)].reshape(8, 32, 128)
+        chunk = unpack_tail(blocks.astype(F32)).reshape(KW, 128).astype(BF)
+        full[k, :, 256:] = chunk
+        hid[:, 256:] += jnp.dot(xk[k], chunk, preferred_element_type=F32)
+        return carry
+
+    lax.fori_loop(0, KC, forward2, 0)
+    activate(2)
+
+    def grads2(k, carry):
+        part = jnp.dot(xt[k], sig[:, 256:], preferred_element_type=F32)
+        blocks = pack_tail(part.reshape(8, ROWS, 128)).astype(BF)
+        zt, y0 = k // 2, lax.rem(k, 2) * 4
+        for j in range(4):
+            ba2[y0 + j, zt] = blocks[2 * j]
+            bb2[zt, y0 + j] = blocks[2 * j + 1]
+        return carry
+
+    lax.fori_loop(0, KC, grads2, 0)
+    g2 = exchange(ba2, bb2, na2, nb2, back2, t1a, t1b, t2, tl_)
+    g2[0]()
 
     def inputs(k, carry):
         term = lax.dot_general(sig[...], full[k], (((1,), (1,)), ((), ())), preferred_element_type=F32)
@@ -295,26 +350,51 @@
         return carry
 
     lax.fori_loop(0, KC, inputs, 0)
-
-    def xcopy(dx):
-        xt_ = lax.rem(x + dx, NX)
+    wide = D // 2
+
+    def target(way, step):
+        return lax.rem(x + 5 - step, NX) if way == 0 else lax.rem(x + NX - 5 + step, NX)
+
+    def shift(way, step, part):
+        lanes = slice(wide * part, wide * part + wide)
         return pltpu.make_async_remote_copy(
-            terms.at[xt_], got.at[x], xs.at[0, dx], xs.at[1, dx], device_id=sdev(zl, xt_), device_id_type=MESH)
-
-    for dx in ORDER_Y:
-        xcopy(dx).start()
-    got[x] = terms[x]
-
-    g_turn_a()
-    g_turn_b()
-    for dx in ORDER_Y:
-        xcopy(dx).wait()
+            terms.at[target(way, step), :, lanes], got.at[way, step - 1, :, lanes],
+            xs.at[0, way, step - 1, part], xs.at[1, way, step - 1, part],
+            device_id=sdev(zl, right if way == 0 else left), device_id_type=MESH)
+
+    def pass_on(way, step, part):
+        shift(way, step - 1, part).wait()
+        to = target(way, step)
+
+        def add(k, carry):
+            lanes = pl.ds(pl.multiple_of(wide * part + k * KW, 128), KW)
+            terms[to, :, lanes] = (
+                terms[to, :, lanes].astype(F32) + got[way, step - 2, :, lanes].astype(F32)).astype(BF)
+            return carry
+
+        lax.fori_loop(0, wide // KW, add, 0)
+        shift(way, step, part).start()
+
+    shift(0, 1, 0).start()
+    shift(1, 1, 1).start()
+    shift(0, 2, 1).start()
+    shift(1, 2, 0).start()
+    pass_on(0, 2, 0)
+    pass_on(1, 2, 1)
+    for way, part in ((0, 1), (1, 0), (0, 0), (1, 1)):
+        pass_on(way, 3, part)
+    g1[1]()
+    g1[2]()
+    for way, part in ((0, 1), (1, 0), (0, 0), (1, 1)):
+        pass_on(way, 4, part)
+    g2[1]()
+    g2[2]()
+    for way, part in ((0, 1), (1, 0), (0, 0), (1, 1)):
+        shift(way, 4, part).wait()
 
     def add_up(k, carry):
         lanes = pl.ds(pl.multiple_of(k * KW, 128), KW)
-        total = got[0, :, lanes].astype(F32)
-        for i in range(1, NX):
-            total = total + got[i, :, lanes].astype(F32)
+        total = terms[x, :, lanes].astype(F32) + got[0, 3, :, lanes].astype(F32) + got[1, 3, :, lanes].astype(F32)
         low, high = total[0:TOK], total[TOK:]
         half[:, lanes] = jnp.where(zl == 0, low, high)
         zsend[:, lanes] = jnp.where(zl == 0, high, low).astype(BF)
@@ -324,56 +404,55 @@
     last = pltpu.make_async_remote_copy(
         zsend, zrecv, ps.at[2], ps.at[3], device_id=sdev(1 - zl, x), device_id_type=MESH)
     last.start()
+
+    def expert_sums(blocks):
+        rows = [blocks[:, :, :, 16 * q:16 * q + 16].reshape(1024, 128) for q in range(2)]
+        total = jnp.dot(pick[...], jnp.concatenate(rows, axis=1), preferred_element_type=F32)
+        return total[:, 0:128].reshape(16, 16, 128), total[:, 128:].reshape(16, 16, 128)
+
+    g1[3]()
+    for pair_of in range(3):
+        sums = expert_sums(back1[:, :, :, 32 * pair_of:32 * pair_of + 32])
+        for i in range(2):
+            q = 2 * pair_of + i
+            grad_out[:, 16 * (q % 3):16 * (q % 3) + 16, 128 * (q // 3):128 * (q // 3) + 128] = sums[i]
     last.wait()
     dx_out[...] = (half[...] + zrecv[...].astype(F32)).astype(BF)
-    g_finish()
-
-
-def sum_kernel(pulled, blocks, out, acc):
-    acc[...] = jnp.zeros(acc.shape, F32)
-
-    def add(k, carry):
-        e = pulled[k]
-        acc[e] = acc[e] + blocks[k].astype(F32)
-        return carry
-
-    lax.fori_loop(0, blocks.shape[0], add, 0)
-
-    def spread(e, carry):
-        total = acc[e]
-        out[e, :, 0:128] = total[0:ROWS]
-        out[e, :, 128:256] = total[ROWS:2 * ROWS]
-        out[e, :, 256:COLS] = unpack_tail(total[None, 96:])[0, :, 0:80]
-        return carry
-
-    lax.fori_loop(0, out.shape[0], spread, 0)
+    g2[3]()
+    low, high = expert_sums(back2[...])
+    grad_out[:, :, 256:] = unpack_tail(jnp.concatenate([low, high], axis=1))[:, :, 0:80]
 
 
 def shards(tokens, route_weight, counts, pulled, weights, cotangent):
     vmem, smem = pl.BlockSpec(memory_space=pltpu.VMEM), pl.BlockSpec(memory_space=pltpu.SMEM)
     dma = pltpu.SemaphoreType.DMA
     route = jnp.broadcast_to(route_weight[:, None], (TOK, 128))
-    activated, input_grads, blocks = pl.pallas_call(
+    hbm = pl.BlockSpec(memory_space=pltpu.HBM)
+
+    def blocks_of(n):
+        outer = [(NY, NZ), (NZ, NY), (NY, NZ), (NZ, NY), (NZ, NY, NC)]
+        return [pltpu.VMEM(shape + (n, 128), BF) for shape in outer]
+
+    sems = [dma((2, NY)), dma((2, NZ)), dma((2, 2 * NY)), dma((3,))]
+    return pl.pallas_call(
         main_kernel,
         out_shape=[
             jax.ShapeDtypeStruct((CAP, COLS), BF),
             jax.ShapeDtypeStruct((TOK, D), BF),
-            jax.ShapeDtypeStruct((NZ, NY, NC, 128, 128), BF),
+            jax.ShapeDtypeStruct(weights.shape, F32),
         ],
-        in_specs=[smem, smem, vmem, vmem, vmem, vmem],
+        in_specs=[smem, smem, hbm, hbm, hbm, hbm],
         out_specs=[vmem, vmem, vmem],
         scratch_shapes=[
-            pltpu.VMEM((16, 128, 128), BF),
-            pltpu.VMEM((NY, NZ, 128, 128), BF),
-            pltpu.VMEM((NZ, NY, 128, 128), BF),
-            pltpu.VMEM((NY, NZ, 128, 128), BF),
-            pltpu.VMEM((NZ, NY, 128, 128), BF),
-            pltpu.VMEM((NZ, NY, NC, 128, 128), BF),
+            pltpu.VMEM((16, ROWS, COLS), BF),
+            pltpu.VMEM((CAP, COLS), BF),
+            pltpu.VMEM((16, 96, 128), BF),
+            pltpu.VMEM((16, 32, 128), BF),
+            *blocks_of(96),
+            *blocks_of(32),
             pltpu.VMEM((KC, KW, 384), BF),
-            pltpu.VMEM((NY, NZ, 128, 128), BF),
-            pltpu.VMEM((NZ, NY, 128, 128), BF),
-            pltpu.VMEM((NY, NZ, 128, 128), BF),
-            pltpu.VMEM((NZ, NY, 128, 128), BF),
+            *blocks_of(96),
+            *blocks_of(32),
             pltpu.VMEM((TOK, D + 128), BF),
             pltpu.VMEM((TOK, D + 128), BF),
             pltpu.VMEM((NX, 2 * TOK, D + 128), BF),
@@ -383,29 +462,19 @@
             pltpu.VMEM((CAP, 384), F32),
             pltpu.VMEM((CAP, 384), F32),
             pltpu.VMEM((CAP, 384), BF),
+            pltpu.VMEM((256, 1024), BF),
             pltpu.VMEM((NX, 2 * TOK, D), BF),
-            pltpu.VMEM((NX, 2 * TOK, D), BF),
+            pltpu.VMEM((2, 4, 2 * TOK, D), BF),
             pltpu.VMEM((TOK, D), BF),
             pltpu.VMEM((TOK, D), BF),
             pltpu.VMEM((TOK, D), F32),
-            dma((2, NY)), dma((2, NZ)), dma((2, 2 * NY)), dma((3,)),
-            dma((2, NY)), dma((2, NZ)), dma((2, 2 * NY)), dma((3,)),
-            dma((4,)), dma((2, 8)), dma((2, NX)),
+            *sems, *sems, *sems, *sems,
+            dma((4,)), dma((2, 8)), dma((2, 2, 4, 2)), dma((4,)),
         ],
         compiler_params=pltpu.CompilerParams(
-            collective_id=1, has_side_effects=True, vmem_limit_bytes=50 << 20),
+            collective_id=1, has_side_effects=True, vmem_limit_bytes=36 << 20),
         name="exchange_and_compute",
     )(pulled, counts, tokens, route, weights, cotangent)
-    weight_grads = pl.pallas_call(
-        sum_kernel,
-        out_shape=jax.ShapeDtypeStruct(weights.shape, F32),
-        in_specs=[smem, vmem],
-        out_specs=vmem,
-        scratch_shapes=[pltpu.VMEM((weights.shape[0], 128, 128), F32)],
-        compiler_params=pltpu.CompilerParams(vmem_limit_bytes=24 << 20),
-        name="sum_per_expert",
-    )(pulled, blocks.reshape(NZ * NY * NC, 128, 128))
-    return activated, input_grads, weight_grads
 
 
 def solution(mesh):

time: 146 us -> 137 us (0.938)
  the two profiles are of different devices: /device:TPU:1 before, /device:TPU:13 now
where the time goes in v2:
time: 137 us
  Pallas kernels  129 us (94%)
  local copies, waits for them, and re-layouts  6.67 us (5%)
    pallas_call x1, Pallas kernels, shards(): pl.pallas_call(main_kernel, out_shape=[jax.ShapeDtypeStruct((CAP, COLS),...  129 us
    unnamed x11, local copies, waits for them, and re-layouts  5.94 us

profile of v2, /device:TPU:13, one launch (start us, length us, event | category | flops | bytes accessed | tf_op | source)
XLA Modules:
  0.0 137.0 jit_solution(17162844978702387487)
XLA Ops:
  1.3 0.7 broadcast_in_dim.2.route_hbm
  2.0 0.0 copy-start
  2.0 1.1 copy-done
  3.1 0.0 copy-start.1
  3.1 0.9 copy-done.1
  4.0 0.0 copy-start.2
  4.0 0.9 copy-done.2
  4.9 0.0 copy-start.3
  4.9 0.7 copy-done.3
  5.6 129.0 %exchange_and_compute.1 = (bf16[320,336]{1,0:T(8,128)(2,1)S(1)}, bf16[20,3072]{1,0:T(8,128)(2,1)S(1)}, f32[16,48,336]{2,1,0:T(8,128)S(1)}) custom-call(s32[64]{0:T(128)S(1)} %copy-done.3, s32[1]{0:T(128)S(6)} %copy.12.counts, bf16[20,3072]{1,0:T(8,128)(2,1)S(1)} %copy-done.2, bf16[20,128]{1,0:T(8,128)(2,1)S(1)} %broadcast_in_dim.2.route_hbm, ...), custom_call_target="tpu_custom_call" | custom-call | tf_op jit(solution)/shard_map/exchange_and_compute/pallas_call | solution.py:437
  134.6 0.7 copy.13
  135.3 0.7 copy.14
  136.0 1.0 copy.15
Async XLA Ops:
  2.0 1.1 copy-start
  3.1 0.9 copy-start.1
  4.0 0.9 copy-start.2
  4.9 0.7 copy-start.3

commit v3 on v2

--- a/solution.py
+++ b/solution.py
@@ -14,8 +14,8 @@
 KC = 8
 KW = D // KC
 BF, F32 = jnp.bfloat16, jnp.float32
-ORDER_Y = (1, 7, 2, 6, 3, 5, 4)
-ORDER_Z = (1, 3, 2)
+ORDER_Y = (4, 3, 5, 2, 6, 1, 7)
+ORDER_Z = (2, 1, 3)
 
 
 def pack_tail(tail):
@@ -37,15 +37,15 @@
 
 
 def main_kernel(
-    pulled, counts, tok_hbm, route_hbm, weights_hbm, cot_hbm,
+    pulled, counts, own_tok, weights, cot,
     act_out, dx_out, grad_out,
-    weights, cot, packed1, packed2,
+    packed1, packed2,
     sa1, sb1, ma1, mb1, land1, sa2, sb2, ma2, mb2, land2, full,
     ba1, bb1, na1, nb1, back1, ba2, bb2, na2, nb2, back2,
-    own_tok, pair_tok, ring, xk, xt, scale, cotp, hid, sig, pick,
+    pair_tok, ring, xk, xt, scale, cotp, hid, sig, pick,
     terms, got, zsend, zrecv, half,
     p1a, p1b, p2, pl_, q1a, q1b, q2, ql_, r1a, r1b, r2, rl_, t1a, t1b, t2, tl_,
-    ps, rg, xs, ins,
+    ps, rg, xs,
 ):
     g, s = lax.axis_index("group"), lax.axis_index("shard")
     zh, y, c = g // 16, lax.rem(g // 2, NY), lax.rem(g, 2)
@@ -56,15 +56,6 @@
 
     def sdev(zl_, x_):
         return (g, zl_ * NX + x_)
-
-    loads = [
-        pltpu.make_async_copy(weights_hbm, weights, ins.at[0]),
-        pltpu.make_async_copy(tok_hbm, own_tok.at[:, 0:D], ins.at[1]),
-        pltpu.make_async_copy(route_hbm, own_tok.at[:, D:], ins.at[2]),
-        pltpu.make_async_copy(cot_hbm, cot, ins.at[3]),
-    ]
-    for load in loads:
-        load.start()
 
     bar = pltpu.get_barrier_semaphore()
 
@@ -82,8 +73,6 @@
         greet(sdev(zl, lax.rem(x + dx, NX)))
     greet(sdev(1 - zl, x))
 
-    loads[0].wait()
-
     def pack_one(e, carry):
         packed1[e] = jnp.concatenate([weights[e, :, 0:128], weights[e, :, 128:256]], axis=0)
         tail = jnp.concatenate([weights[e, :, 256:].astype(F32), jnp.zeros((ROWS, 384 - COLS), F32)], axis=1)
@@ -101,8 +90,6 @@
         return carry
 
     lax.fori_loop(0, NZ * NY, fill, 0)
-    loads[1].wait()
-    loads[2].wait()
 
     pl.semaphore_wait(bar, 29)
 
@@ -134,13 +121,19 @@
         l2a = pltpu.make_async_copy(ia.at[:, zh], dst.at[zh, :, 0], sl.at[2])
         l2b = pltpu.make_async_copy(ib.at[:, y], dst.at[:, y, 1], sl.at[2])
 
-        def start1():
+        def start_b(dz):
+            b1(dz).start()
+
+        def start_a():
             la.start()
             lb.start()
-            for i, dy in enumerate(ORDER_Y):
+            for dy in ORDER_Y:
                 a1(dy).start()
-                if i % 2 == 0 and i // 2 < 3:
-                    b1(ORDER_Z[i // 2]).start()
+
+        def start1():
+            for dz in ORDER_Z:
+                start_b(dz)
+            start_a()
 
         def turn_a():
             la.wait()
@@ -195,7 +188,7 @@
                 for dz in ORDER_Z + (0,):
                     a2(dz, 1).wait_send()
 
-        return start1, turn_a, turn_b, finish
+        return start1, turn_a, turn_b, finish, start_a, start_b
 
     pair = pltpu.make_async_remote_copy(
         own_tok, pair_tok, ps.at[0], ps.at[1], device_id=sdev(1 - zl, x), device_id_type=MESH)
@@ -236,7 +229,6 @@
             copy.wait()
 
     hop_start(1)
-    loads[3].wait()
     cotp[:, 256:] = jnp.zeros((CAP, 128), F32)
     cotp[:, 0:COLS] = cot[...].astype(F32)
 
@@ -312,9 +304,13 @@
             bb1[zt, y0 + j, ROWS:] = high[2 * j + 1]
         return carry
 
-    lax.fori_loop(0, KC, grads1, 0)
     g1 = exchange(ba1, bb1, na1, nb1, back1, r1a, r1b, r2, rl_)
-    g1[0]()
+    for dz in ORDER_Z + (0,):
+        zt_ = lax.rem(zh + dz, NZ)
+        lax.fori_loop(0, 2, lambda i, carry: grads1(2 * zt_ + i, carry), 0)
+        if dz:
+            g1[5](dz)
+    g1[4]()
 
     w2[3]()
 
@@ -426,9 +422,8 @@
 def shards(tokens, route_weight, counts, pulled, weights, cotangent):
     vmem, smem = pl.BlockSpec(memory_space=pltpu.VMEM), pl.BlockSpec(memory_space=pltpu.SMEM)
     dma = pltpu.SemaphoreType.DMA
-    route = jnp.broadcast_to(route_weight[:, None], (TOK, 128))
-    hbm = pl.BlockSpec(memory_space=pltpu.HBM)
-
+    lane = lax.broadcasted_iota(jnp.int32, (TOK, D + 128), 1)
+    both = jnp.where(lane < D, jnp.pad(tokens, ((0, 0), (0, 128))), route_weight[:, None])
     def blocks_of(n):
         outer = [(NY, NZ), (NZ, NY), (NY, NZ), (NZ, NY), (NZ, NY, NC)]
         return [pltpu.VMEM(shape + (n, 128), BF) for shape in outer]
@@ -441,11 +436,9 @@
             jax.ShapeDtypeStruct((TOK, D), BF),
             jax.ShapeDtypeStruct(weights.shape, F32),
         ],
-        in_specs=[smem, smem, hbm, hbm, hbm, hbm],
+        in_specs=[smem, smem, vmem, vmem, vmem],
         out_specs=[vmem, vmem, vmem],
         scratch_shapes=[
-            pltpu.VMEM((16, ROWS, COLS), BF),
-            pltpu.VMEM((CAP, COLS), BF),
             pltpu.VMEM((16, 96, 128), BF),
             pltpu.VMEM((16, 32, 128), BF),
             *blocks_of(96),
@@ -453,7 +446,6 @@
             pltpu.VMEM((KC, KW, 384), BF),
             *blocks_of(96),
             *blocks_of(32),
-            pltpu.VMEM((TOK, D + 128), BF),
             pltpu.VMEM((TOK, D + 128), BF),
             pltpu.VMEM((NX, 2 * TOK, D + 128), BF),
             pltpu.VMEM((KC, CAP, KW), BF),
@@ -469,12 +461,12 @@
             pltpu.VMEM((TOK, D), BF),
             pltpu.VMEM((TOK, D), F32),
             *sems, *sems, *sems, *sems,
-            dma((4,)), dma((2, 8)), dma((2, 2, 4, 2)), dma((4,)),
+            dma((4,)), dma((2, 8)), dma((2, 2, 4, 2)),
         ],
         compiler_params=pltpu.CompilerParams(
             collective_id=1, has_side_effects=True, vmem_limit_bytes=36 << 20),
         name="exchange_and_compute",
-    )(pulled, counts, tokens, route, weights, cotangent)
+    )(pulled, counts, both, weights, cotangent)
 
 
 def solution(mesh):

time: 137 us -> 132 us (0.964)
  the two profiles are of different devices: /device:TPU:13 before, /device:TPU:1 now
where the time goes in v3:
time: 132 us
  Pallas kernels  125 us (95%)
  local copies, waits for them, and re-layouts  5.03 us (4%)
    pallas_call x1, Pallas kernels, shards(): pl.pallas_call(main_kernel, out_shape=[jax.ShapeDtypeStruct((CAP, COLS),...  125 us
    unnamed x9, local copies, waits for them, and re-layouts  5.03 us

profile of v3, /device:TPU:1, one launch (start us, length us, event | category | flops | bytes accessed | tf_op | source)
XLA Modules:
  0.0 132.0 jit_solution(13209296364333588728)
XLA Ops:
  1.3 1.0 pad_select_fusion.own_tok
  2.3 0.0 copy-start
  2.3 1.1 copy-done
  3.4 0.0 copy-start.1
  3.4 0.9 copy-done.1
  4.3 0.0 copy-start.2
  4.3 0.7 copy-done.2
  5.0 124.7 %exchange_and_compute.1 = (bf16[320,336]{1,0:T(8,128)(2,1)S(1)}, bf16[20,3072]{1,0:T(8,128)(2,1)S(1)}, f32[16,48,336]{2,1,0:T(8,128)S(1)}) custom-call(s32[64]{0:T(128)S(1)} %copy-done.2, s32[1]{0:T(128)S(6)} %copy.12.counts, bf16[20,3200]{1,0:T(8,128)(2,1)S(1)} %pad_select_fusion.own_tok, bf16[16,48,336]{2,1,0:T(8,128)(2,1)S(1)} %copy-done, ...), custom_call_target="tpu_custom_call" | custom-call | tf_op jit(solution)/shard_map/exchange_and_compute/pallas_call | solution.py:432
  129.7 0.7 copy.13
  130.4 0.7 copy.14
  131.0 1.0 copy.15
  (1 shorter events, 0.0 us)
Async XLA Ops:
  2.3 1.1 copy-start
  3.4 0.9 copy-start.1
  4.3 0.7 copy-start.2

commit v4 on v3

--- a/solution.py
+++ b/solution.py
@@ -73,24 +73,11 @@
         greet(sdev(zl, lax.rem(x + dx, NX)))
     greet(sdev(1 - zl, x))
 
-    def pack_one(e, carry):
+    def pack_main(e, carry):
         packed1[e] = jnp.concatenate([weights[e, :, 0:128], weights[e, :, 128:256]], axis=0)
-        tail = jnp.concatenate([weights[e, :, 256:].astype(F32), jnp.zeros((ROWS, 384 - COLS), F32)], axis=1)
-        packed2[e] = pack_tail(tail[None])[0].astype(BF)
-        return carry
-
-    lax.fori_loop(0, weights.shape[0], pack_one, 0)
-
-    def fill(k, carry):
-        zt, yt = k // NY, lax.rem(k, NY)
-        sa1[yt, zt] = packed1[pulled[2 * k]]
-        sb1[zt, yt] = packed1[pulled[2 * k + 1]]
-        sa2[yt, zt] = packed2[pulled[2 * k]]
-        sb2[zt, yt] = packed2[pulled[2 * k + 1]]
-        return carry
-
-    lax.fori_loop(0, NZ * NY, fill, 0)
-
+        return carry
+
+    lax.fori_loop(0, weights.shape[0], pack_main, 0)
     pl.semaphore_wait(bar, 29)
 
     def exchange(src_a, src_b, ia, ib, dst, s1a, s1b, s2, sl):
@@ -195,7 +182,35 @@
     pair.start()
     w1 = exchange(sa1, sb1, ma1, mb1, land1, p1a, p1b, p2, pl_)
     w2 = exchange(sa2, sb2, ma2, mb2, land2, q1a, q1b, q2, ql_)
-    w1[0]()
+
+    def fill_b(zt, yt, carry):
+        sb1[zt, yt] = packed1[pulled[2 * (zt * NY + yt) + 1]]
+        return carry
+
+    def fill_a(k, carry):
+        sa1[lax.rem(k, NY), k // NY] = packed1[pulled[2 * k]]
+        return carry
+
+    for dz in ORDER_Z + (0,):
+        lax.fori_loop(0, NY, functools.partial(fill_b, lax.rem(zh + dz, NZ)), 0)
+        if dz:
+            w1[5](dz)
+    lax.fori_loop(0, NZ * NY, fill_a, 0)
+    w1[4]()
+
+    def pack_rest(e, carry):
+        tail = jnp.concatenate([weights[e, :, 256:].astype(F32), jnp.zeros((ROWS, 384 - COLS), F32)], axis=1)
+        packed2[e] = pack_tail(tail[None])[0].astype(BF)
+        return carry
+
+    def fill_rest(k, carry):
+        zt, yt = k // NY, lax.rem(k, NY)
+        sa2[yt, zt] = packed2[pulled[2 * k]]
+        sb2[zt, yt] = packed2[pulled[2 * k + 1]]
+        return carry
+
+    lax.fori_loop(0, weights.shape[0], pack_rest, 0)
+    lax.fori_loop(0, NZ * NY, fill_rest, 0)
     w2[0]()
 
     pair.wait()

time: 132 us -> 131 us (level)
  no operation moved by 1% of the time
where the time goes in v4:
time: 131 us
  Pallas kernels  124 us (95%)
  local copies, waits for them, and re-layouts  5.03 us (4%)
  between operations  1.31 us (1%)
    pallas_call x1, Pallas kernels, shards(): pl.pallas_call(main_kernel, out_shape=[jax.ShapeDtypeStruct((CAP, COLS),...  124 us
    unnamed x9, local copies, waits for them, and re-layouts  5.03 us

profile of v4, /device:TPU:1, one launch (start us, length us, event | category | flops | bytes accessed | tf_op | source)
XLA Modules:
  0.0 131.2 jit_solution(10899893949585742277)
XLA Ops:
  1.3 1.0 pad_select_fusion.own_tok
  2.3 0.0 copy-start
  2.3 1.1 copy-done
  3.4 0.0 copy-start.1
  3.4 0.9 copy-done.1
  4.3 0.0 copy-start.2
  4.3 0.7 copy-done.2
  5.0 123.8 %exchange_and_compute.1 = (bf16[320,336]{1,0:T(8,128)(2,1)S(1)}, bf16[20,3072]{1,0:T(8,128)(2,1)S(1)}, f32[16,48,336]{2,1,0:T(8,128)S(1)}) custom-call(s32[64]{0:T(128)S(1)} %copy-done.2, s32[1]{0:T(128)S(6)} %copy.12.counts, bf16[20,3200]{1,0:T(8,128)(2,1)S(1)} %pad_select_fusion.own_tok, bf16[16,48,336]{2,1,0:T(8,128)(2,1)S(1)} %copy-done, ...), custom_call_target="tpu_custom_call" | custom-call | tf_op jit(solution)/shard_map/exchange_and_compute/pallas_call | solution.py:447
  128.8 0.7 copy.13
  129.5 0.7 copy.14
  130.1 1.0 copy.15
  (1 shorter events, 0.0 us)
Async XLA Ops:
  2.3 1.1 copy-start
  3.4 0.9 copy-start.1
  4.3 0.7 copy-start.2
